TPU v7x, 256 devices: a whole 4x4x8 slice. The times are simulated.
256 devices in a mesh: leaf: 16 (over x, y), row: 16 (over z, core).
Axes of the slice: x: 4, y: 4, z: 8, core: 2. Of those that a mesh axis runs over, the one named last changes fastest.
Arguments:
- rhs: bfloat16 [6, 16, 512, 256], P(None, 'leaf', 'row'), may hold values from -6 to 6
- diag_inverse: bfloat16 [16, 6, 512, 512], P('leaf'), as said below
- factor: bfloat16 [16, 178, 512, 512], P('leaf', None, 'row'), as said below
- widths: int32 [6, 16], P(None, 'leaf'), may hold values from 64 to 512, as said below
- structure: int32 [16, 178], P('leaf'), may hold values from 0 to 1, as said below
Outputs:
- forward_solution: bfloat16 [6, 16, 512, 256], P(None, 'leaf', 'row')
- adjoint_solution: bfloat16 [6, 16, 512, 256], P(None, 'leaf', 'row')
Inputs may be any that keep to these rules, and one draw needn't show every extreme that they name: `widths`: every draw has a supernode of exactly 512 columns and one of exactly one eighth of 512 columns. `structure`: 1 where the block is present. Each diag_inverse[j, l] is lower triangular with diagonal entries from 0.5 to 1. `factor`: dense blocks of independent entries.
All inputs are finite; a program needn't handle non-finite values.
Results may differ from a plain program's by a relative error of at most 0.017.
Values may be sent and summed in bfloat16 or wider, within the bound.
A program may use at most 64 MiB of HBM per device.

v0:
```python
import jax
import jax.numpy as jnp
from jax import lax
from jax.sharding import PartitionSpec as P


def group_size(level_now, leaf_count):
    return min(2**level_now, leaf_count)


def block_offsets(levels, leaf_count):
    offset_table = {}
    cursor = 0
    for source_level in range(levels):
        for target_level in range(source_level + 1, levels):
            offset_table[source_level, target_level] = cursor
            cursor += group_size(target_level, leaf_count)
    return offset_table


def blocks_after(level_now, levels, leaf_count):
    return sum(
        (group_size(target_level, leaf_count) for target_level in range(level_now + 1, levels))
    )


def contract_rows(left_side, right_side):
    return lax.dot_general(
        left_side, right_side, (((0,), (0,)), ((), ())), preferred_element_type=jnp.float32
    )


def apply_columns(matrix, shard_piece):
    return jnp.dot(matrix, shard_piece, preferred_element_type=jnp.float32)


def group_reduce(partials, group_span, leaf_count, leaf_index):
    group_base = leaf_index // group_span * group_span
    spread = jnp.zeros((leaf_count,) + partials.shape[1:], jnp.float32)
    spread = lax.dynamic_update_slice_in_dim(spread, partials, group_base, 0)
    return lax.psum_scatter(
        spread.astype(jnp.bfloat16), "leaf", scatter_dimension=0, tiled=True
    ).astype(jnp.float32)[0]


def group_collect(own_block, group_span, leaf_index):
    everyone = lax.all_gather(own_block[None], "leaf", axis=0, tiled=True)
    group_base = leaf_index // group_span * group_span
    return lax.dynamic_slice_in_dim(everyone, group_base, group_span, 0)


def adjoint_level(flat_blocks, flat_values, own_full, full_mask, block_mask, inverse_cols):
    pulled = lax.psum(contract_rows(flat_blocks, flat_values).astype(jnp.bfloat16), "row").astype(
        jnp.float32
    )
    reduced_full = (full_mask[:, None] * (own_full.astype(jnp.float32) - pulled)).astype(
        jnp.bfloat16
    )
    solved = contract_rows(inverse_cols, reduced_full)
    return (block_mask[:, None] * solved).astype(jnp.bfloat16)


def shards(rhs, diag_inverse, factor, widths, structure):
    leaf_count = lax.axis_size("leaf")
    leaf_index = lax.axis_index("leaf")
    row_index = lax.axis_index("row")
    levels = rhs.shape[0]
    block_rows = rhs.shape[2]
    columns = rhs.shape[3]
    full_width = factor.shape[3]
    inverse = diag_inverse[0]
    blocks = factor[0]
    weights = structure[0].astype(jnp.float32)
    own_rows = row_index * block_rows
    positions = jnp.arange(full_width, dtype=jnp.int32)
    full_masks = (positions[None, :] < widths).astype(jnp.float32)
    block_masks = lax.dynamic_slice_in_dim(full_masks, own_rows, block_rows, 1)
    offset_table = block_offsets(levels, leaf_count)
    pending = {}
    for target_level in range(1, levels):
        pending[target_level] = jnp.zeros(
            (group_size(target_level, leaf_count), block_rows, columns), jnp.float32
        )
    forward_blocks = []
    forward_full = []
    for level_now in range(levels):
        if level_now > 0:
            incoming = group_reduce(
                pending[level_now], group_size(level_now, leaf_count), leaf_count, leaf_index
            )
        else:
            incoming = jnp.zeros((block_rows, columns), jnp.float32)
        residual = (
            block_masks[level_now][:, None] * (rhs[level_now, 0].astype(jnp.float32) - incoming)
        ).astype(jnp.bfloat16)
        solve_rows = inverse[level_now]
        folded = apply_columns(solve_rows, lax.all_gather(residual, "row", axis=0, tiled=True))
        solved_full = (full_masks[level_now][:, None] * folded).astype(jnp.bfloat16)
        solved_block = lax.dynamic_slice_in_dim(solved_full, own_rows, block_rows, 0)
        forward_blocks.append(solved_block)
        forward_full.append(solved_full)
        if level_now + 1 < levels:
            first_block = offset_table[level_now, level_now + 1]
            block_count = blocks_after(level_now, levels, leaf_count)
            chosen = blocks[first_block : first_block + block_count].reshape(
                block_count * block_rows, full_width
            )
            products = jnp.dot(chosen, solved_full, preferred_element_type=jnp.float32).reshape(
                block_count, block_rows, columns
            )
            products = products * weights[first_block : first_block + block_count][:, None, None]
            cursor = 0
            for target_level in range(level_now + 1, levels):
                group_span = group_size(target_level, leaf_count)
                pending[target_level] = (
                    pending[target_level] + products[cursor : cursor + group_span]
                )
                cursor += group_span
    gathered = {}
    adjoint_blocks = [None] * levels
    for level_now in reversed(range(levels)):
        inverse_cols = lax.dynamic_slice_in_dim(inverse[level_now], own_rows, block_rows, 1)
        if level_now + 1 == levels:
            solved = contract_rows(inverse_cols, forward_full[level_now])
            own_adjoint = (block_masks[level_now][:, None] * solved).astype(jnp.bfloat16)
        else:
            first_block = offset_table[level_now, level_now + 1]
            block_count = blocks_after(level_now, levels, leaf_count)
            stacked = jnp.concatenate(
                [gathered[upper_level] for upper_level in range(level_now + 1, levels)], 0
            )
            stacked = stacked * structure[0, first_block : first_block + block_count][
                :, None, None
            ].astype(jnp.bfloat16)
            flat_blocks = blocks[first_block : first_block + block_count].reshape(
                block_count * block_rows, full_width
            )
            flat_values = stacked.reshape(block_count * block_rows, columns)
            own_adjoint = adjoint_level(
                flat_blocks,
                flat_values,
                forward_full[level_now],
                full_masks[level_now],
                block_masks[level_now],
                inverse_cols,
            )
        adjoint_blocks[level_now] = own_adjoint
        if level_now > 0:
            gathered[level_now] = group_collect(
                own_adjoint, group_size(level_now, leaf_count), leaf_index
            )
    return (jnp.stack(forward_blocks)[:, None], jnp.stack(adjoint_blocks)[:, None])


def solution(mesh):
    placed = (
        P(None, "leaf", "row", None),
        P("leaf", None, None, None),
        P("leaf", None, "row", None),
        P(None, "leaf"),
        P("leaf", None),
    )
    return jax.shard_map(
        shards,
        mesh=mesh,
        in_specs=placed,
        out_specs=(P(None, "leaf", "row", None), P(None, "leaf", "row", None)),
        check_vma=False,
    )
```

profile of v0, /device:TPU:1, one launch (start us, length us, event | category | flops | bytes accessed | tf_op | source)
XLA Modules:
  0.0 1223.9 jit_solution(11152830773635222627)
XLA Ops:
  8.9 22.0 %all_gather.33 = bf16[512,256]{1,0:T(8,128)(2,1)S(1)} all-gather(bf16[32,256]{1,0:T(8,128)(2,1)S(1)} %fusion.72), channel_id=1, replica_groups=mesh['leaf'=16,'row'=16] {'row'}, dimensions={0}, use_global_device_ids=true | all-gather | bytes 278528 | tf_op jit(solution)/shard_map/all_gather | solution.py:97
  30.9 1.6 slice.219
  32.6 1.4 fusion
  34.9 1.1 copy-done
  36.8 1.5 slice.228
  38.4 71.6 %reduce-scatter.16.cloned.1.call-done = bf16[1,32,256]{2,1,0:T(8,128)(2,1)} async-done(((bf16[16,32,256]{2,1,0:T(8,128)(2,1)}), bf16[1,32,256]{2,1,0:T(8,128)(2,1)}) %reduce-scatter.16.cloned.1.call-update) | async-done | bytes 16400
  110.8 20.2 %all_gather.34 = bf16[512,256]{1,0:T(8,128)(2,1)S(1)} all-gather(bf16[32,256]{1,0:T(8,128)(2,1)S(1)} %fusion.71), channel_id=1, replica_groups=mesh['leaf'=16,'row'=16] {'row'}, dimensions={0}, use_global_device_ids=true | all-gather | bytes 278528 | tf_op jit(solution)/shard_map/all_gather | solution.py:97
  131.0 1.4 fusion.1
  133.1 1.7 convolution_bitcast_fusion.1
  134.8 2.9 copy.19
  137.7 1.5 broadcast_multiply_fusion.1
  139.3 1.1 copy-done.1
  142.1 2.5 slice.238
  144.7 69.2 %reduce-scatter.18.cloned.1.call-done = bf16[1,32,256]{2,1,0:T(8,128)(2,1)} async-done(((bf16[16,32,256]{2,1,0:T(8,128)(2,1)}), bf16[1,32,256]{2,1,0:T(8,128)(2,1)}) %reduce-scatter.18.cloned.1.call-update) | async-done | bytes 16400
  214.8 20.3 %all_gather.35 = bf16[512,256]{1,0:T(8,128)(2,1)S(1)} all-gather(bf16[32,256]{1,0:T(8,128)(2,1)S(1)} %fusion.69), channel_id=1, replica_groups=mesh['leaf'=16,'row'=16] {'row'}, dimensions={0}, use_global_device_ids=true | all-gather | bytes 278528 | tf_op jit(solution)/shard_map/all_gather | solution.py:97
  235.1 1.4 fusion.2
  237.2 1.6 convolution_bitcast_fusion
  238.8 2.8 copy.20
  241.6 1.5 broadcast_multiply_fusion.2
  246.0 2.3 slice.249
  248.5 69.3 %reduce-scatter.20.cloned.1.call-done = bf16[1,32,256]{2,1,0:T(8,128)(2,1)} async-done(((bf16[16,32,256]{2,1,0:T(8,128)(2,1)}), bf16[1,32,256]{2,1,0:T(8,128)(2,1)}) %reduce-scatter.20.cloned.1.call-update) | async-done | bytes 16400
  318.6 20.2 %all_gather.36 = bf16[512,256]{1,0:T(8,128)(2,1)S(1)} all-gather(bf16[32,256]{1,0:T(8,128)(2,1)S(1)} %fusion.67), channel_id=1, replica_groups=mesh['leaf'=16,'row'=16] {'row'}, dimensions={0}, use_global_device_ids=true | all-gather | bytes 278528 | tf_op jit(solution)/shard_map/all_gather | solution.py:97
  338.9 1.4 fusion.3
  341.0 1.5 convolution_bitcast_fusion.2
  342.5 2.6 copy.21
  345.1 1.4 broadcast_multiply_fusion.3
  347.5 2.2 fusion.21
  352.1 69.4 %reduce-scatter.22.cloned.1.call-done = bf16[1,32,256]{2,1,0:T(8,128)(2,1)} async-done(((bf16[16,32,256]{2,1,0:T(8,128)(2,1)}), bf16[1,32,256]{2,1,0:T(8,128)(2,1)}) %reduce-scatter.22.cloned.1.call-update) | async-done | bytes 16400
  422.3 20.3 %all_gather.37 = bf16[512,256]{1,0:T(8,128)(2,1)S(1)} all-gather(bf16[32,256]{1,0:T(8,128)(2,1)S(1)} %fusion.65), channel_id=1, replica_groups=mesh['leaf'=16,'row'=16] {'row'}, dimensions={0}, use_global_device_ids=true | all-gather | bytes 278528 | tf_op jit(solution)/shard_map/all_gather | solution.py:97
  442.6 1.4 fusion.4
  444.7 1.2 convolution_bitcast_fusion.3
  445.9 2.1 copy.22
  448.0 2.5 fusion.20
  451.1 3.5 fusion.86
  454.7 67.7 %reduce-scatter.24.cloned.1.call-done = bf16[1,32,256]{2,1,0:T(8,128)(2,1)} async-done(((bf16[16,32,256]{2,1,0:T(8,128)(2,1)}), bf16[1,32,256]{2,1,0:T(8,128)(2,1)}) %reduce-scatter.24.cloned.1.call-update) | async-done | bytes 16400
  523.2 20.2 %all_gather.38 = bf16[512,256]{1,0:T(8,128)(2,1)S(1)} all-gather(bf16[32,256]{1,0:T(8,128)(2,1)S(1)} %fusion.63), channel_id=1, replica_groups=mesh['leaf'=16,'row'=16] {'row'}, dimensions={0}, use_global_device_ids=true | all-gather | bytes 278528 | tf_op jit(solution)/shard_map/all_gather | solution.py:97
  543.4 1.4 fusion.5
  544.8 1.2 fusion.11
  546.1 18.0 %all-gather = bf16[512,256]{1,0:T(8,128)(2,1)S(1)} all-gather(bf16[32,256]{1,0:T(8,128)(2,1)S(1)} %fusion.11), channel_id=2, replica_groups=mesh['leaf'=16,'row'=16] {'leaf'}, dimensions={0}, use_global_device_ids=true | all-gather | bytes 278528 | tf_op jit(solution)/shard_map/all_gather | solution.py:47
  565.9 1.6 dynamic-slice_bitcast_fusion.4
  567.5 1.5 copy.23
  569.0 105.7 %all-reduce.11.cloned.1.call-done = bf16[512,256]{0,1:T(8,128)(2,1)} async-done(((bf16[512,256]{0,1:T(8,128)(2,1)}), bf16[512,256]{0,1:T(8,128)(2,1)}) %all-reduce.11.cloned.1.call-update) | async-done | bytes 262160 | tf_op jit(solution)/shard_map/psum | solution.py:53
  674.7 1.3 fusion.12
  676.1 18.5 %all-gather.1 = bf16[512,256]{1,0:T(8,128)(2,1)S(1)} all-gather(bf16[32,256]{1,0:T(8,128)(2,1)S(1)} %fusion.12), channel_id=3, replica_groups=mesh['leaf'=16,'row'=16] {'leaf'}, dimensions={0}, use_global_device_ids=true | all-gather | bytes 278528 | tf_op jit(solution)/shard_map/all_gather | solution.py:47
  695.3 1.2 fusion.8
  696.6 1.3 constant_dynamic-update-slice_fusion.5
  698.6 1.3 constant_dynamic-update-slice_fusion.4
  699.9 109.0 %all-reduce.13.cloned.1.call-done = bf16[512,256]{0,1:T(8,128)(2,1)} async-done(((bf16[512,256]{0,1:T(8,128)(2,1)}), bf16[512,256]{0,1:T(8,128)(2,1)}) %all-reduce.13.cloned.1.call-update) | async-done | bytes 262160 | tf_op jit(solution)/shard_map/psum | solution.py:53
  808.9 1.5 fusion.13
  810.4 18.5 %all-gather.2 = bf16[512,256]{1,0:T(8,128)(2,1)S(1)} all-gather(bf16[32,256]{1,0:T(8,128)(2,1)S(1)} %fusion.13), channel_id=4, replica_groups=mesh['leaf'=16,'row'=16] {'leaf'}, dimensions={0}, use_global_device_ids=true | all-gather | bytes 278528 | tf_op jit(solution)/shard_map/all_gather | solution.py:47
  831.0 1.2 fusion.9
  832.3 1.6 dynamic-slice_bitcast_fusion.2
  833.9 1.5 copy.25
  836.1 1.3 constant_dynamic-update-slice_fusion.3
  837.5 107.2 %all-reduce.15.cloned.1.call-done = bf16[512,256]{0,1:T(8,128)(2,1)} async-done(((bf16[512,256]{0,1:T(8,128)(2,1)}), bf16[512,256]{0,1:T(8,128)(2,1)}) %all-reduce.15.cloned.1.call-update) | async-done | bytes 262160 | tf_op jit(solution)/shard_map/psum | solution.py:53
  944.7 1.4 fusion.14
  946.1 18.7 %all-gather.3 = bf16[512,256]{1,0:T(8,128)(2,1)S(1)} all-gather(bf16[32,256]{1,0:T(8,128)(2,1)S(1)} %fusion.14), channel_id=5, replica_groups=mesh['leaf'=16,'row'=16] {'leaf'}, dimensions={0}, use_global_device_ids=true | all-gather | bytes 278528 | tf_op jit(solution)/shard_map/all_gather | solution.py:47
  966.6 1.3 fusion.10
  969.6 110.7 %all-reduce.17.cloned.1.call-done = bf16[512,256]{0,1:T(8,128)(2,1)} async-done(((bf16[512,256]{0,1:T(8,128)(2,1)}), bf16[512,256]{0,1:T(8,128)(2,1)}) %all-reduce.17.cloned.1.call-update) | async-done | bytes 262160 | tf_op jit(solution)/shard_map/psum | solution.py:53
  1080.3 1.3 fusion.15
  1081.7 18.5 %all-gather.4 = bf16[512,256]{1,0:T(8,128)(2,1)S(1)} all-gather(bf16[32,256]{1,0:T(8,128)(2,1)S(1)} %fusion.15), channel_id=6, replica_groups=mesh['leaf'=16,'row'=16] {'leaf'}, dimensions={0}, use_global_device_ids=true | all-gather | bytes 278528 | tf_op jit(solution)/shard_map/all_gather | solution.py:47
  1101.3 1.3 fusion.7
  1103.9 111.1 %all-reduce.19.cloned.1.call-done = bf16[512,256]{0,1:T(8,128)(2,1)} async-done(((bf16[512,256]{0,1:T(8,128)(2,1)}), bf16[512,256]{0,1:T(8,128)(2,1)}) %all-reduce.19.cloned.1.call-update) | async-done | bytes 262160 | tf_op jit(solution)/shard_map/psum | solution.py:53
  1215.0 1.3 fusion.18
  (170 shorter events, 31.9 us)
Async XLA Ops:
  7.2 102.8 %reduce-scatter.16.cloned.1.call-start = ((), (), s32[]{:S(2)}) async-start(), calls=%async_computation.10 | async-start | bytes 278528
  8.0 24.6 %copy-start.31 = (f32[1,512]{1,0:T(1,128)}, f32[1,512]{1,0:T(1,128)S(1)}, u32[]{:S(2)}) copy-start(f32[1,512]{1,0:T(1,128)S(1)} %get-tuple-element.19) | copy-start | bytes 6148
  8.0 123.0 %copy-start.33 = (f32[1,512]{1,0:T(1,128)}, f32[1,512]{1,0:T(1,128)S(1)}, u32[]{:S(2)}) copy-start(f32[1,512]{1,0:T(1,128)S(1)} %get-tuple-element.18) | copy-start | bytes 6148
  8.0 227.1 %copy-start.35 = (f32[1,512]{1,0:T(1,128)}, f32[1,512]{1,0:T(1,128)S(1)}, u32[]{:S(2)}) copy-start(f32[1,512]{1,0:T(1,128)S(1)} %get-tuple-element.17) | copy-start | bytes 6148
  8.0 330.9 %copy-start.36 = (f32[1,512]{1,0:T(1,128)}, f32[1,512]{1,0:T(1,128)S(1)}, u32[]{:S(2)}) copy-start(f32[1,512]{1,0:T(1,128)S(1)} %get-tuple-element.16) | copy-start | bytes 6148
  8.0 434.6 %copy-start.37 = (f32[1,512]{1,0:T(1,128)}, f32[1,512]{1,0:T(1,128)S(1)}, u32[]{:S(2)}) copy-start(f32[1,512]{1,0:T(1,128)S(1)} %get-tuple-element.15) | copy-start | bytes 6148
  8.1 0.8 copy-start.38
  8.1 101.9 %copy-start.40 = (f32[32]{0:T(128)}, f32[32]{0:T(128)S(1)}, u32[]{:S(2)}) copy-start(f32[32]{0:T(128)S(1)} %get-tuple-element.24) | copy-start | bytes 388
  8.1 205.8 %copy-start.42 = (f32[32]{0:T(128)}, f32[32]{0:T(128)S(1)}, u32[]{:S(2)}) copy-start(f32[32]{0:T(128)S(1)} %get-tuple-element.23) | copy-start | bytes 388
  8.1 309.6 %copy-start.43 = (f32[32]{0:T(128)}, f32[32]{0:T(128)S(1)}, u32[]{:S(2)}) copy-start(f32[32]{0:T(128)S(1)} %get-tuple-element.22) | copy-start | bytes 388
  8.1 413.4 %copy-start.44 = (f32[32]{0:T(128)}, f32[32]{0:T(128)S(1)}, u32[]{:S(2)}) copy-start(f32[32]{0:T(128)S(1)} %get-tuple-element.21) | copy-start | bytes 388
  30.9 1.6 copy-start.46
  34.0 0.7 copy-start.10
  34.8 1.2 copy-start
  36.0 0.7 copy-start.21
  36.7 73.2 %copy-start.29 = (bf16[6,1,32,256]{3,2,1,0:T(8,128)(2,1)S(1)}, bf16[6,1,32,256]{3,2,1,0:T(8,128)(2,1)}, u32[]{:S(2)}) copy-start(bf16[6,1,32,256]{3,2,1,0:T(8,128)(2,1)} %param.5) | copy-start | bytes 294916
  36.7 177.2 %reduce-scatter.18.cloned.1.call-start = ((), (), s32[]{:S(2)}) async-start(), calls=%async_computation.11 | async-start | bytes 278528
  132.4 0.7 copy-start.12
  139.3 1.1 copy-start.1
  141.3 0.7 copy-start.22
  142.0 175.7 %reduce-scatter.20.cloned.1.call-start = ((), (), s32[]{:S(2)}) async-start(), calls=%async_computation.12 | async-start | bytes 278528
  213.9 23.3 %copy-start.2 = (bf16[1,40,32,512]{3,2,1,0:T(8,128)(2,1)S(1)}, bf16[1,40,32,512]{3,2,1,0:T(8,128)(2,1)}, u32[]{:S(2)}) copy-start(bf16[1,40,32,512]{3,2,1,0:T(8,128)(2,1)} %slice.238) | copy-start | bytes 3932164
  236.4 0.7 copy-start.16
  243.1 1.1 copy-start.4
  245.2 0.7 copy-start.20
  245.9 175.6 %reduce-scatter.22.cloned.1.call-start = ((), (), s32[]{:S(2)}) async-start(), calls=%async_computation.13 | async-start | bytes 278528
  317.7 23.2 %copy-start.7 = (bf16[1,32,32,512]{3,2,1,0:T(8,128)(2,1)S(1)}, bf16[1,32,32,512]{3,2,1,0:T(8,128)(2,1)}, u32[]{:S(2)}) copy-start(bf16[1,32,32,512]{3,2,1,0:T(8,128)(2,1)} %slice.249) | copy-start | bytes 3145732
  340.3 0.7 copy-start.15
  346.4 1.0 copy-start.9
  349.7 172.6 %reduce-scatter.24.cloned.1.call-start = ((), (), s32[]{:S(2)}) async-start(), calls=%async_computation.14 | async-start | bytes 278528
  350.9 95.0 %copy-start.5 = (bf16[1,16,32,512]{3,2,1,0:T(8,128)(2,1)}, bf16[1,16,32,512]{3,2,1,0:T(8,128)(2,1)S(1)}, u32[]{:S(2)}) copy-start(bf16[1,16,32,512]{3,2,1,0:T(8,128)(2,1)S(1)} %slice.261) | copy-start | bytes 1572868
  444.0 0.7 copy-start.13
  450.5 224.2 %all-reduce.11.cloned.1.call-start = ((), (), s32[]{:S(2)}) async-start(), calls=%async_computation.5 | async-start | bytes 524288 | tf_op jit(solution)/shard_map/psum | solution.py:53
  522.3 41.9 %copy-start.6 = (bf16[1,16,32,512]{3,2,1,0:T(8,128)(2,1)S(1)}, bf16[1,16,32,512]{3,2,1,0:T(8,128)(2,1)}, u32[]{:S(2)}) copy-start(bf16[1,16,32,512]{3,2,1,0:T(8,128)(2,1)} %copy-done.5) | copy-start | bytes 1572868
  544.8 19.2 %copy-start.24 = (bf16[256,512]{1,0:T(8,128)(2,1)}, bf16[256,512]{1,0:T(8,128)(2,1)S(1)}, u32[]{:S(2)}) copy-start(bf16[256,512]{1,0:T(8,128)(2,1)S(1)} %fusion.5) | copy-start | bytes 786436
  544.8 129.9 %copy-start.14 = (bf16[256,512]{1,0:T(8,128)(2,1)S(1)}, bf16[256,512]{1,0:T(8,128)(2,1)}, u32[]{:S(2)}) copy-start(bf16[256,512]{1,0:T(8,128)(2,1)} %copy-done.13) | copy-start | bytes 786436
  565.2 243.7 %all-reduce.13.cloned.1.call-start = ((), (), s32[]{:S(2)}) async-start(), calls=%async_computation.6 | async-start | bytes 524288 | tf_op jit(solution)/shard_map/psum | solution.py:53
  674.7 20.6 %copy-start.8 = (bf16[1,32,32,512]{3,2,1,0:T(8,128)(2,1)S(1)}, bf16[1,32,32,512]{3,2,1,0:T(8,128)(2,1)}, u32[]{:S(2)}) copy-start(bf16[1,32,32,512]{3,2,1,0:T(8,128)(2,1)} %slice.249) | copy-start | bytes 3145732
  676.1 18.5 %copy-start.25 = (bf16[32,256]{1,0:T(8,128)(2,1)}, bf16[32,256]{1,0:T(8,128)(2,1)S(1)}, u32[]{:S(2)}) copy-start(bf16[32,256]{1,0:T(8,128)(2,1)S(1)} %fusion.12) | copy-start | bytes 49156
  696.5 248.2 %all-reduce.15.cloned.1.call-start = ((), (), s32[]{:S(2)}) async-start(), calls=%async_computation.7 | async-start | bytes 524288 | tf_op jit(solution)/shard_map/psum | solution.py:53
  808.9 22.1 %copy-start.3 = (bf16[1,40,32,512]{3,2,1,0:T(8,128)(2,1)S(1)}, bf16[1,40,32,512]{3,2,1,0:T(8,128)(2,1)}, u32[]{:S(2)}) copy-start(bf16[1,40,32,512]{3,2,1,0:T(8,128)(2,1)} %slice.238) | copy-start | bytes 3932164
  810.4 21.8 %copy-start.27 = (bf16[32,256]{1,0:T(8,128)(2,1)}, bf16[32,256]{1,0:T(8,128)(2,1)S(1)}, u32[]{:S(2)}) copy-start(bf16[32,256]{1,0:T(8,128)(2,1)S(1)} %fusion.13) | copy-start | bytes 49156
  829.0 0.7 copy-start.18
  829.7 0.6 copy-start.17
  832.3 248.0 %all-reduce.17.cloned.1.call-start = ((), (), s32[]{:S(2)}) async-start(), calls=%async_computation.8 | async-start | bytes 524288 | tf_op jit(solution)/shard_map/psum | solution.py:53
  964.8 0.7 copy-start.23
  966.5 1.4 copy-start.30
  966.5 113.7 %copy-start.34 = (f32[1,512]{1,0:T(1,128)S(1)}, f32[1,512]{1,0:T(1,128)}, u32[]{:S(2)}) copy-start(f32[1,512]{1,0:T(1,128)} %copy-done.33) | copy-start | bytes 6148
  966.5 113.7 %copy-start.41 = (f32[32]{0:T(128)S(1)}, f32[32]{0:T(128)}, u32[]{:S(2)}) copy-start(f32[32]{0:T(128)} %copy-done.40) | copy-start | bytes 388
  967.8 133.2 %copy-start.19 = (bf16[512,256]{1,0:T(8,128)(2,1)S(1)}, bf16[512,256]{1,0:T(8,128)(2,1)}, u32[]{:S(2)}) copy-start(bf16[512,256]{1,0:T(8,128)(2,1)} %copy-done.18) | copy-start | bytes 786436
  967.9 133.2 %copy-start.47 = (bf16[46]{0:T(256)(128)(2,1)S(1)}, bf16[46]{0:T(256)(128)(2,1)}, u32[]{:S(2)}) copy-start(bf16[46]{0:T(256)(128)(2,1)} %slice_bitcast_fusion) | copy-start | bytes 280
  967.9 247.1 %all-reduce.19.cloned.1.call-start = ((), (), s32[]{:S(2)}) async-start(), calls=%async_computation.9 | async-start | bytes 524288 | tf_op jit(solution)/shard_map/psum | solution.py:53
  1101.2 113.8 %copy-start.11 = (bf16[256,512]{1,0:T(8,128)(2,1)S(1)}, bf16[256,512]{1,0:T(8,128)(2,1)}, u32[]{:S(2)}) copy-start(bf16[256,512]{1,0:T(8,128)(2,1)} %copy-done.10) | copy-start | bytes 786436
  1101.2 113.8 %copy-start.32 = (f32[1,512]{1,0:T(1,128)S(1)}, f32[1,512]{1,0:T(1,128)}, u32[]{:S(2)}) copy-start(f32[1,512]{1,0:T(1,128)} %copy-done.31) | copy-start | bytes 6148
  1101.3 113.8 %copy-start.39 = (f32[32]{0:T(128)S(1)}, f32[32]{0:T(128)}, u32[]{:S(2)}) copy-start(f32[32]{0:T(128)} %copy-done.38) | copy-start | bytes 388
  1101.3 115.1 %copy-start.28 = (bf16[32,256]{1,0:T(8,128)(2,1)S(1)}, bf16[32,256]{1,0:T(8,128)(2,1)}, u32[]{:S(2)}) copy-start(bf16[32,256]{1,0:T(8,128)(2,1)} %copy-done.27) | copy-start | bytes 49156
  1101.3 115.1 %copy-start.26 = (bf16[32,256]{1,0:T(8,128)(2,1)S(1)}, bf16[32,256]{1,0:T(8,128)(2,1)}, u32[]{:S(2)}) copy-start(bf16[32,256]{1,0:T(8,128)(2,1)} %copy-done.25) | copy-start | bytes 49156
  1216.4 0.6 copy-start.45
Sparse Core Ops, SparseCore 0:
  36.8 73.0 reduce-scatter.15
  142.2 71.6 reduce-scatter.17
  246.1 71.6 reduce-scatter.19
  349.8 71.6 reduce-scatter.21
  450.6 71.6 reduce-scatter.23
  565.4 109.3 all-reduce.10
  696.6 112.2 all-reduce.12
  832.4 112.2 all-reduce.14
  968.0 112.2 all-reduce.16
  1102.7 112.2 all-reduce.18
where the time goes:
time: 1230 us; the launch traced here: 1220 us
  waiting for transfers between devices  891 us (72%)
  blocking collectives  215 us (17%)
  local copies, waits for them, and re-layouts  53.4 us (4%)
  matrix products  29 us (2%)
  other arithmetic  19.6 us (2%)
  between operations  15 us (1%)
    psum x5, waiting for transfers between devices, adjoint_level(): lax.psum(contract_rows(flat_blocks, flat_values).astype(jnp.bfloat16), 'r...  544 us
    unnamed x15, waiting for transfers between devices  347 us
    all_gather x6, blocking collectives, shards(): lax.all_gather(residual, 'row', axis=0, tiled=True)  123 us
    all_gather x5, blocking collectives, group_collect(): everyone = lax.all_gather(own_block[None], 'leaf', axis=0, tiled=True)  92.2 us
  transfers between devices with their start and end apart: 10, of which 10 were waited for; matrix products, arithmetic and copies ran while one was open for 2% of the time, Pallas kernels for 0%

commit v1 on v0

v1 whole, which is shorter than its diff:
```python
import functools
import jax
import jax.numpy as jnp
from jax import lax
from jax.experimental import pallas as pl
from jax.experimental.pallas import tpu as pltpu
from jax.sharding import PartitionSpec as P

MESH = pl.DeviceIdType.MESH
F32 = jnp.float32
BF16 = jnp.bfloat16
LEVELS = 6
LEAVES = 16
ROWS = 32
WIDTH = 512
COLUMNS = 256
STREAMS = 1
PART = COLUMNS // STREAMS
TARGETS = tuple(range(1, LEVELS))


def group_size(level):
    return min(2**level, LEAVES)


def block_offsets():
    table, cursor = {}, 0
    for source in range(LEVELS):
        for target in range(source + 1, LEVELS):
            table[source, target] = cursor
            cursor += group_size(target)
    return table


OFFSETS = block_offsets()
BLOCKS = sum(group_size(t) * t for t in TARGETS)


def dot(a, b):
    return jnp.dot(a, b, preferred_element_type=F32)


def dot_nt(a, b):
    return lax.dot_general(a, b, (((1,), (1,)), ((), ())), preferred_element_type=F32)


ROW_Z, ROW_SIB, LEAF, B_LEAF, B_SIB, B_Z = (i * LEVELS for i in range(6))
SLOTS = 6 * LEVELS


def kernel(rhs, diag, factor, widths, structure, fwd, adj, *scratch):
    scratch = list(scratch)

    def take(n):
        out = scratch[:n]
        del scratch[:n]
        return out

    per_target = lambda: dict(zip(TARGETS, take(len(TARGETS))))
    blocks, fold, fold_t = per_target(), per_target(), per_target()
    dm, dm_t, twice = take(3)
    pre, part_out, part_in = per_target(), per_target(), per_target()
    resid = take(1)[0]
    gathered = per_target()
    pulled_pre, pulled_out, pulled_sib, pair_out, pair_in, head = take(6)
    send_sem, recv_sem, load_sem = take(3)

    leaf = lax.axis_index("leaf")
    row = lax.axis_index("row")
    z, core = row // 2, lax.rem(row, 2)
    sibling = z * 2 + (1 - core)
    other = 1 - core
    own = pl.ds(pl.multiple_of(row * ROWS, ROWS), ROWS)

    diag_load = pltpu.make_async_copy(diag.at[0], dm, load_sem.at[0])
    diag_load.start()
    loads = {}
    for i, t in enumerate(TARGETS):
        for s in range(t):
            loads[s, t] = pltpu.make_async_copy(
                factor.at[0, pl.ds(OFFSETS[s, t], group_size(t))],
                blocks[t].at[s],
                load_sem.at[1 + len(loads)],
            )
            loads[s, t].start()

    barrier = pltpu.get_barrier_semaphore()

    def greet(leaf_to, row_to):
        pl.semaphore_signal(barrier, inc=1, device_id=(leaf_to, row_to), device_id_type=MESH)

    for k in range(1, LEAVES):
        greet(lax.rem(leaf + k, LEAVES), row)
    for k in range(1, 8):
        greet(leaf, lax.rem(z + k, 8) * 2 + core)
    greet(leaf, sibling)
    pl.semaphore_wait(barrier, LEAVES + 7)

    sends = []

    def send(src, dst, st, slot, leaf_to, row_to):
        pltpu.make_async_remote_copy(
            src_ref=src,
            dst_ref=dst,
            send_sem=send_sem.at[st, slot],
            recv_sem=recv_sem.at[st, slot],
            device_id=(leaf_to, row_to),
            device_id_type=MESH,
        ).start()

    def wait(sem, st, slot, ref):
        pltpu.make_async_copy(ref, ref, sem.at[st, slot]).wait()

    def receive(st, slot, ref):
        wait(recv_sem, st, slot, ref)
        sends.append((st, slot, ref))

    def members(level):
        span = group_size(level)
        base = leaf // span * span
        return span, base, leaf - base

    def row_mask(level, first, count):
        rows = first + lax.broadcasted_iota(jnp.int32, (count, 1), 0)
        return (rows < widths[level, 0]).astype(F32)

    def cols(st):
        return pl.ds(st * PART, PART)

    def prepare_diag(s):
        if s == 0:
            diag_load.wait()
        masked = (dm[s].astype(F32) * row_mask(s, 0, WIDTH)).astype(BF16)
        dm[s] = masked
        dm_t[s] = masked.T.reshape(8, 2, ROWS, WIDTH)
        twice[s] = dot(dm_t[s, z, core], masked).astype(BF16)

    def load_blocks(t):
        for s in range(t):
            loads[s, t].wait()
        span = group_size(t)

        def scale(i, carry):
            s, p = i // span, lax.rem(i, span)
            first = OFFSETS[0, t]
            for later in range(1, t):
                first = jnp.where(s == later, OFFSETS[later, t], first)
            w = structure[0, first + p].astype(F32)
            blocks[t][s, p] = (blocks[t][s, p].astype(F32) * w).astype(BF16)
            return carry

        lax.fori_loop(0, t * span, scale, 0)

    def prepare_fold(t):
        load_blocks(t)
        span = group_size(t)

        def step(s, carry):
            flat = blocks[t][s].reshape(span * ROWS, WIDTH)
            for c in range(2):
                fold[t][s, c] = dot_nt(flat, dm_t[s, :, c].reshape(256, WIDTH)).astype(BF16)
            return carry

        lax.fori_loop(0, t, step, 0)

    def prepare_fold_t(t):
        span = group_size(t)

        def step(s, carry):
            flat = blocks[t][s].reshape(span * ROWS, WIDTH)
            for c in range(2):
                product = dot_nt(dm_t[s, :, c].reshape(256, WIDTH), flat)
                fold_t[t][s, c] = product.astype(BF16)
            return carry

        lax.fori_loop(0, t, step, 0)

    def half(st, level, c):
        return resid[st, level, :, c].reshape(256, PART)

    def prepare_pre(st, t):
        total = None
        for s in range(t - 1):
            for c in range(2):
                term = dot(fold[t][s, c], half(st, s, c))
                total = term if total is None else total + term
        if total is not None:
            pre[t][st] = total

    def outputs(st, level):
        full = resid[st, level].reshape(WIDTH, PART)
        fwd[level, 0, :, cols(st)] = dot(dm[level, own], full).astype(BF16)
        head[st, level] = dot(twice[level], full)

    def prepare_pulled(st, s):
        for c in range(2):
            total = None
            for t in range(s + 2, LEVELS):
                k = group_size(t) * ROWS
                term = dot(fold_t[t][s, c], gathered[t][st].reshape(k, PART))
                total = term if total is None else total + term
            if total is not None:
                pulled_pre[st, s, c] = total

    def send_gathered(st, level, block):
        span, base, me = members(level)
        gathered[level][st, me] = block
        for k in range(1, span):
            send(
                gathered[level].at[st, me],
                gathered[level].at[st, me],
                st,
                B_LEAF + level,
                base + lax.rem(me + k, span),
                row,
            )

    def stream(st):
        for level in range(LEVELS):
            value = rhs[level, 0, :, cols(st)].astype(F32)
            if level > 0:
                span, base, me = members(level)
                yield "leaf", level
                receive(st, LEAF + level, part_in[level].at[st, pl.ds(0, span - 1)])
                update = jnp.sum(part_in[level][st].astype(F32), axis=0)
                value = value - update
            resid[st, level, z, core] = (value * row_mask(level, row * ROWS, ROWS)).astype(BF16)
            for k in (4, 3, 5, 2, 6, 1, 7):
                send(
                    resid.at[st, level, z, core],
                    resid.at[st, level, z, core],
                    st,
                    ROW_Z + level,
                    leaf,
                    lax.rem(z + k, 8) * 2 + core,
                )
            yield "row_z", level
            receive(st, ROW_Z + level, resid.at[st, level, pl.ds(0, 7), 0])
            send(
                resid.at[st, level, :, core],
                resid.at[st, level, :, core],
                st,
                ROW_SIB + level,
                leaf,
                sibling,
            )
            target = level + 1
            if target < LEVELS:
                total = dot(fold[target][level, core], half(st, level, core))
                if target > 1:
                    total = total + pre[target][st]
                pre[target][st] = total
            yield "row_sib", level
            receive(st, ROW_SIB + level, resid.at[st, level, :, 0])
            if target < LEVELS:
                span, base, me = members(target)
                total = pre[target][st] + dot(
                    fold[target][level, other], half(st, level, other)
                )
                part_out[target][st] = total.astype(BF16).reshape(span, ROWS, PART)
                for k in range(1, span):
                    to = lax.rem(me + k, span)
                    send(
                        part_out[target].at[st, to],
                        part_in[target].at[st, me],
                        st,
                        LEAF + target,
                        base + to,
                        row,
                    )
                part_in[target][st, me] = part_out[target][st, me]
        top = LEVELS - 1
        solved = dot(twice[top], resid[st, top].reshape(WIDTH, PART))
        block = (solved * row_mask(top, row * ROWS, ROWS)).astype(BF16)
        adj[top, 0, :, cols(st)] = block
        send_gathered(st, top, block)
        for level in reversed(range(top)):
            span, base, me = members(level + 1)
            yield "b_leaf", level
            receive(st, B_LEAF + level + 1, gathered[level + 1].at[st, pl.ds(0, span - 1)])

            def pulled(c):
                values = gathered[level + 1][st].reshape(span * ROWS, PART)
                total = dot(fold_t[level + 1][level, c], values)
                if level + 2 < LEVELS:
                    total = total + pulled_pre[st, level, c]
                return total

            pulled_out[st, level] = pulled(other).astype(BF16).reshape(8, ROWS, PART)
            send(
                pulled_out.at[st, level],
                pulled_sib.at[st, level],
                st,
                B_SIB + level,
                leaf,
                sibling,
            )
            pulled_pre[st, level, core] = pulled(core)
            yield "b_sib", level
            receive(st, B_SIB + level, pulled_sib.at[st, level])
            pair = pulled_pre[st, level, core].reshape(8, ROWS, PART) + pulled_sib[
                st, level
            ].astype(F32)
            pair_out[st, level] = pair.astype(BF16)
            for k in (4, 3, 5, 2, 6, 1, 7):
                to = lax.rem(z + k, 8)
                send(
                    pair_out.at[st, level, to],
                    pair_in.at[st, level, z],
                    st,
                    B_Z + level,
                    leaf,
                    to * 2 + core,
                )
            pair_in[st, level, z] = pair_out[st, level, z]
            yield "b_z", level
            receive(st, B_Z + level, pair_in.at[st, level, pl.ds(0, 7)])
            total = jnp.sum(pair_in[st, level].astype(F32), axis=0)
            block = ((head[st, level] - total) * row_mask(level, row * ROWS, ROWS)).astype(BF16)
            adj[level, 0, :, cols(st)] = block
            if level > 0:
                send_gathered(st, level, block)

    def shared_work(kind, level):
        if kind == "row_z":
            if level == 0:
                prepare_diag(0)
                prepare_fold(1)
            elif level < LEVELS - 1:
                prepare_fold(level + 1)
            else:
                prepare_fold_t(LEVELS - 2)
        elif kind == "leaf":
            prepare_diag(level)
            if level == LEVELS - 1:
                prepare_fold_t(LEVELS - 1)
            elif level > 1:
                prepare_fold_t(level - 1)

    def stream_work(st, kind, level):
        if kind == "row_z":
            if 0 < level < LEVELS - 1:
                prepare_pre(st, level + 1)
        elif kind == "leaf":
            outputs(st, level - 1)
        elif kind == "b_leaf" and level == LEVELS - 2:
            outputs(st, LEVELS - 1)
        elif kind == "b_z" and level > 0:
            prepare_pulled(st, level - 1)

    running = [(st, stream(st)) for st in range(STREAMS)]
    while running:
        for st, steps in list(running):
            step = next(steps, None)
            if step is None:
                running.remove((st, steps))
                continue
            if st == 0:
                shared_work(*step)
            stream_work(st, *step)
    for st, slot, ref in sends:
        wait(send_sem, st, slot, ref)


def scratch_shapes():
    vmem = pltpu.VMEM
    shapes = []
    shapes += [vmem((t, group_size(t), ROWS, WIDTH), BF16) for t in TARGETS]
    shapes += [vmem((t, 2, group_size(t) * ROWS, 256), BF16) for t in TARGETS]
    shapes += [vmem((t, 2, 256, group_size(t) * ROWS), BF16) for t in TARGETS]
    shapes += [
        vmem((LEVELS, WIDTH, WIDTH), BF16),
        vmem((LEVELS, 8, 2, ROWS, WIDTH), BF16),
        vmem((LEVELS, ROWS, WIDTH), BF16),
    ]
    shapes += [vmem((STREAMS, group_size(t) * ROWS, PART), F32) for t in TARGETS]
    shapes += [vmem((STREAMS, group_size(t), ROWS, PART), BF16) for t in TARGETS]
    shapes += [vmem((STREAMS, group_size(t), ROWS, PART), BF16) for t in TARGETS]
    shapes += [vmem((STREAMS, LEVELS, 8, 2, ROWS, PART), BF16)]
    shapes += [vmem((STREAMS, group_size(t), ROWS, PART), BF16) for t in TARGETS]
    shapes += [vmem((STREAMS, LEVELS - 1, 2, 256, PART), F32)]
    shapes += [vmem((STREAMS, LEVELS - 1, 8, ROWS, PART), BF16) for _ in range(4)]
    shapes += [vmem((STREAMS, LEVELS, ROWS, PART), F32)]
    shapes += [
        pltpu.SemaphoreType.DMA((STREAMS, SLOTS)),
        pltpu.SemaphoreType.DMA((STREAMS, SLOTS)),
        pltpu.SemaphoreType.DMA((16,)),
    ]
    return shapes


def shards(rhs, diag_inverse, factor, widths, structure):
    out = jax.ShapeDtypeStruct((LEVELS, 1, ROWS, COLUMNS), BF16)
    return pl.pallas_call(
        kernel,
        out_shape=(out, out),
        in_specs=[
            pl.BlockSpec(memory_space=pltpu.VMEM),
            pl.BlockSpec(memory_space=pl.ANY),
            pl.BlockSpec(memory_space=pl.ANY),
            pl.BlockSpec(memory_space=pltpu.SMEM),
            pl.BlockSpec(memory_space=pltpu.SMEM),
        ],
        out_specs=(
            pl.BlockSpec(memory_space=pltpu.VMEM),
            pl.BlockSpec(memory_space=pltpu.VMEM),
        ),
        scratch_shapes=scratch_shapes(),
        compiler_params=pltpu.CompilerParams(
            collective_id=0, has_side_effects=True, vmem_limit_bytes=52 * 2**20
        ),
    )(rhs, diag_inverse, factor, widths, structure)


def solution(mesh):
    placed = (
        P(None, "leaf", "row", None),
        P("leaf", None, None, None),
        P("leaf", None, "row", None),
        P(None, "leaf"),
        P("leaf", None),
    )
    return jax.shard_map(
        shards,
        mesh=mesh,
        in_specs=placed,
        out_specs=(P(None, "leaf", "row", None), P(None, "leaf", "row", None)),
        check_vma=False,
    )
```

time: 1230 us -> 134 us (0.11)
  waiting for transfers between devices: 891 us -> 0 us
  blocking collectives: 215 us -> 0 us
  Pallas kernels: 0 us -> 130 us
  local copies, waits for them, and re-layouts: 53.4 us -> 3.6 us
  matrix products: 29 us -> 0 us
  other arithmetic: 19.6 us -> 0 us
  between operations: 15 us -> 0.64 us
    psum x5 -> x0, waiting for transfers between devices: 544 us -> none  [adjoint_level(): lax.psum(contract_rows(flat_blocks, flat_values).astype(jnp.bfloat16), 'r...]
    unnamed x15 -> x0, waiting for transfers between devices: 347 us -> none
    all_gather x11 -> x0, blocking collectives: 215 us -> none  [the longest x6 123 us: shards(): lax.all_gather(residual, 'row', axis=0, tiled=True)]
    pallas_call x0 -> x1, Pallas kernels: none -> 130 us  [shards(): pl.pallas_call(kernel, out_shape=(out, out), in_specs=[pl.BlockSpec(memor...]
    dot_general x22 -> x0, matrix products: 29 us -> none  [the longest x11 14.1 us: contract_rows(): lax.dot_general(left_side, right_side, (((0,), (0,)), ((), ())), preferre...]
    unnamed x109 -> x7, local copies, waits for them, and re-layouts: 18.2 us -> 3.6 us
    slice x12 -> x0, local copies, waits for them, and re-layouts: 12.8 us -> none  [the longest x5 9.02 us: shards(): blocks[first_block:first_block + block_count]]
  transfers between devices with their start and end apart: 10 -> 0, of which waited for: 10 -> 0; matrix products, arithmetic and copies ran while one was open for 2% -> 0% of each run, Pallas kernels for 0% -> 0%
where the time goes in v1:
time: 134 us
  Pallas kernels  130 us (97%)
  local copies, waits for them, and re-layouts  3.6 us (3%)
    pallas_call x1, Pallas kernels, shards(): pl.pallas_call(kernel, out_shape=(out, out), in_specs=[pl.BlockSpec(memor...  130 us
    unnamed x7, local copies, waits for them, and re-layouts  3.6 us

profile of v1, /device:TPU:1, one launch (start us, length us, event | category | flops | bytes accessed | tf_op | source)
XLA Modules:
  0.0 133.9 jit_solution(9604867104050917866)
XLA Ops:
  0.6 0.7 copy.7.widths
  1.4 0.0 copy-start
  1.4 0.9 copy-done
  2.3 0.0 copy-start.1
  2.3 0.7 copy-done.1
  2.9 129.7 %shard_map.68 = (bf16[6,1,32,256]{3,2,1,0:T(8,128)(2,1)S(1)}, bf16[6,1,32,256]{3,2,1,0:T(8,128)(2,1)S(1)}) custom-call(bf16[6,1,32,256]{3,2,1,0:T(8,128)(2,1)S(1)} %copy-done, bf16[1,6,512,512]{3,2,1,0:T(8,128)(2,1)} %diag.1, bf16[1,178,32,512]{3,2,1,0:T(8,128)(2,1)} %factor.1, s32[6,1]{1,0:T(8,128)S(1)} %copy.7.widths, s32[1,178]{1,0:T(1,128)S(1)} %copy-done.1), custom_call_target="tpu_custom_call" | custom-call | tf_op jit(solution)/shard_map/pallas_call | solution.py:394
  132.7 0.6 copy.10
  133.3 0.6 copy.11
Async XLA Ops:
  1.4 0.9 copy-start
  2.3 0.7 copy-start.1

commit v2 on v1

v2 whole, which is shorter than its diff:
```python
import jax
import jax.numpy as jnp
from jax import lax
from jax.experimental import pallas as pl
from jax.experimental.pallas import tpu as pltpu
from jax.sharding import PartitionSpec as P

MESH = pl.DeviceIdType.MESH
F32 = jnp.float32
BF16 = jnp.bfloat16
LEVELS = 6
LEAVES = 16
CHIPS = 8
ROWS = 32
PAIR = 2 * ROWS
WIDTH = 512
COLUMNS = 256
PART = COLUMNS // 2
TARGETS = tuple(range(1, LEVELS))
TOP = LEVELS - 1
FAR_FIRST = (4, 3, 5, 2, 6, 1, 7)


def group_size(level):
    return min(2**level, LEAVES)


def block_offsets():
    table, cursor = {}, 0
    for source in range(LEVELS):
        for target in range(source + 1, LEVELS):
            table[source, target] = cursor
            cursor += group_size(target)
    return table


OFFSETS = block_offsets()


def dot(a, b):
    return jnp.dot(a, b, preferred_element_type=F32)


def dot_nt(a, b):
    return lax.dot_general(a, b, (((1,), (1,)), ((), ())), preferred_element_type=F32)


ROW_Z, LEAF, B_LEAF, B_Z, FOLD, FOLD_T = (i * LEVELS for i in range(6))
RHS_X, FWD_X, HEAD_X = (6 * LEVELS + i for i in range(3))
SLOTS = 6 * LEVELS + 3


def kernel(rhs_hbm, diag, factor, widths_hbm, structure_hbm, fwd, adj, *scratch):
    scratch = list(scratch)

    def take(n):
        out = scratch[:n]
        del scratch[:n]
        return out

    per_target = lambda: dict(zip(TARGETS, take(len(TARGETS))))
    blocks, fold, fold_t = per_target(), per_target(), per_target()
    dm, dm_t, twice = take(3)
    pre, part_out, part_in = per_target(), per_target(), per_target()
    (resid,) = take(1)
    gathered = per_target()
    pulled_pre, pair_out, pair_in, head = take(4)
    rhs, rhs_out, rhs_in, fwd_out, fwd_in, head_in, first_out = take(7)
    widths, structure = take(2)
    send_sem, recv_sem, load_sem = take(3)

    leaf = lax.axis_index("leaf")
    row = lax.axis_index("row")
    z, core = row // 2, lax.rem(row, 2)
    other = 1 - core
    sibling = z * 2 + other
    quarter = z // 2

    loads = {}

    def load(name, src, dst):
        loads[name] = pltpu.make_async_copy(src, dst, load_sem.at[len(loads)])
        loads[name].start()

    load("widths", widths_hbm, widths)
    load("rhs", rhs_hbm.at[:, 0], rhs)
    load("structure", structure_hbm, structure)
    load("diag", diag.at[0], dm)
    for t in TARGETS:
        for s in range(t):
            load((s, t), factor.at[0, pl.ds(OFFSETS[s, t], group_size(t))], blocks[t].at[s])

    barrier = pltpu.get_barrier_semaphore()

    def greet(leaf_to, row_to):
        pl.semaphore_signal(barrier, inc=1, device_id=(leaf_to, row_to), device_id_type=MESH)

    for k in FAR_FIRST:
        for c in range(2):
            greet(leaf, lax.rem(z + k, CHIPS) * 2 + c)
    greet(leaf, sibling)
    for k in range(1, LEAVES):
        greet(lax.rem(leaf + k, LEAVES), row)

    sends = []

    def send(src, dst, slot, leaf_to, row_to):
        pltpu.make_async_remote_copy(
            src_ref=src,
            dst_ref=dst,
            send_sem=send_sem.at[slot],
            recv_sem=recv_sem.at[slot],
            device_id=(leaf_to, row_to),
            device_id_type=MESH,
        ).start()

    def wait(sem, slot, ref):
        pltpu.make_async_copy(ref, ref, sem.at[slot]).wait()

    def receive(slot, ref):
        wait(recv_sem, slot, ref)
        sends.append((slot, ref))

    def members(level):
        span = group_size(level)
        base = leaf // span * span
        return span, base, leaf - base

    def row_mask(level, first, count):
        rows = first + lax.broadcasted_iota(jnp.int32, (count, 1), 0)
        return (rows < widths[level]).astype(F32)

    def pair_mask(level):
        return row_mask(level, z * PAIR, PAIR)

    def prepare_diag(s):
        masked = (dm[s].astype(F32) * row_mask(s, 0, WIDTH)).astype(BF16)
        dm[s] = masked
        dm_t[s] = masked.T.reshape(CHIPS, PAIR, WIDTH)
        twice[s] = dot(dm_t[s, z], masked).astype(BF16)

    def load_blocks(t):
        for s in range(t):
            loads[s, t].wait()
        span = group_size(t)

        def scale(i, carry):
            s, p = i // span, lax.rem(i, span)
            first = OFFSETS[0, t]
            for later in range(1, t):
                first = jnp.where(s == later, OFFSETS[later, t], first)
            w = structure[0, first + p].astype(F32)
            blocks[t][s, p] = (blocks[t][s, p].astype(F32) * w).astype(BF16)
            return carry

        lax.fori_loop(0, t * span, scale, 0)

    def prepare_fold(t):
        load_blocks(t)
        span = group_size(t)

        def step(s, carry):
            flat = blocks[t][s].reshape(span * ROWS, WIDTH)
            for c in range(2):
                cols = pl.ds(c * 256, 256)
                part = dot_nt(flat, dm_t[s, pl.ds(c * 4, 4)].reshape(256, WIDTH))
                fold[t][s, :, core, :, cols] = part.astype(BF16).reshape(span, ROWS, 256)
            return carry

        lax.fori_loop(0, t, step, 0)
        mine = fold[t].at[:, :, core]
        send(mine, mine, FOLD + t, leaf, sibling)

    def prepare_fold_t(t):
        span = group_size(t)

        def step(s, carry):
            flat = blocks[t][s].reshape(span * ROWS, WIDTH)
            for c in range(2):
                part = dot_nt(dm_t[s, pl.ds(c * 4, 4)].reshape(256, WIDTH), flat)
                fold_t[t][s, core, pl.ds(c * 2, 2)] = part.astype(BF16).reshape(
                    2, 128, span * ROWS
                )
            return carry

        lax.fori_loop(0, t, step, 0)
        mine = fold_t[t].at[:, core]
        send(mine, mine, FOLD_T + t, leaf, sibling)

    def full(level):
        return resid[level].reshape(WIDTH, PART)

    def prepare_pre(t):
        receive(FOLD + t, fold[t].at[:, :, 0])
        height = group_size(t) * PAIR
        if t > 1:
            total = None
            for s in range(t - 1):
                term = dot(fold[t][s].reshape(height, WIDTH), full(s))
                total = term if total is None else total + term
            pre[t][...] = total.reshape(group_size(t), PAIR, PART)

    def outputs(level):
        rows = pl.ds(pl.multiple_of(z * PAIR, PAIR), PAIR)
        fwd_out[level] = dot(dm[level, rows], full(level)).astype(BF16).reshape(2, ROWS, PART)
        head[level] = dot(twice[level], full(level)).reshape(2, ROWS, PART)

    def prepare_pulled(s):
        total = None
        for t in range(s + 2, LEVELS):
            k = group_size(t) * ROWS
            for b in range(2):
                term = dot(
                    fold_t[t][s, b].reshape(WIDTH, k), gathered[t][b].reshape(k, PART)
                )
                total = term if total is None else total + term
        pulled_pre[s] = total.reshape(4, 128, PART)

    def send_gathered(level, block):
        span, base, me = members(level)
        gathered[level][:, me] = block
        mine = gathered[level].at[:, me]
        for to in neighbours(span, me):
            send(mine, mine, B_LEAF + level, base + to, row)

    def grid_of(span):
        deep = min(span, 4)
        return span // deep, deep

    ORDER = {1: (0,), 2: (1, 0), 4: (2, 1, 3, 0)}

    def neighbours(span, me):
        wide, deep = grid_of(span)
        for dx in ORDER[wide]:
            for dy in ORDER[deep]:
                if dx or dy:
                    x = lax.rem(me // deep + dx, wide)
                    yield x * deep + lax.rem(lax.rem(me, deep) + dy, deep)

    loads["widths"].wait()
    loads["rhs"].wait()
    first = (rhs[0].astype(F32) * row_mask(0, row * ROWS, ROWS)).astype(BF16)
    for c in range(2):
        first_out[c] = first[:, c * PART : (c + 1) * PART]
        rhs_out[c] = rhs[:, :, c * PART : (c + 1) * PART]
    mine = pl.ds(pl.multiple_of(core * ROWS, ROWS), ROWS)
    resid[0, z, mine] = first_out[core]
    pl.semaphore_wait(barrier, LEAVES + 14)
    for k in FAR_FIRST:
        for c in range(2):
            send(
                first_out.at[c],
                resid.at[0, z, mine],
                ROW_Z,
                leaf,
                lax.rem(z + k, CHIPS) * 2 + c,
            )
    send(first_out.at[other], resid.at[0, z, mine], ROW_Z, leaf, sibling)
    send(rhs_out.at[other], rhs_in.at[core], RHS_X, leaf, sibling)
    rhs_in[core] = rhs_out[core]

    for level in range(LEVELS):
        if level > 0:
            span, base, me = members(level)
            receive(LEAF + level, part_in[level].at[pl.ds(0, span - 1)])
            update = jnp.sum(part_in[level][...].astype(F32), axis=0)
            value = rhs_in[:, level].reshape(PAIR, PART).astype(F32) - update
            resid[level, z] = (value * pair_mask(level)).astype(BF16)
            for k in FAR_FIRST:
                send(
                    resid.at[level, z],
                    resid.at[level, z],
                    ROW_Z + level,
                    leaf,
                    lax.rem(z + k, CHIPS) * 2 + core,
                )
        if level == 0:
            loads["diag"].wait()
            loads["structure"].wait()
            prepare_diag(0)
            prepare_fold(1)
            prepare_diag(1)
            prepare_fold(2)
        elif level == 1:
            prepare_diag(3)
            prepare_fold(4)
        elif level == 2:
            prepare_fold(5)
        elif level == 3:
            prepare_fold_t(4)
        elif level == 4:
            prepare_fold_t(3)
        else:
            outputs(4)
            head_mine = head.at[0, other]
            send(head_mine, head_in, HEAD_X, leaf, sibling)
        if level < TOP:
            prepare_pre(level + 1)
        if level == 0:
            receive(ROW_Z, resid.at[pl.ds(0, 5), pl.ds(0, 3), pl.ds(0, ROWS)])
        else:
            receive(ROW_Z + level, resid.at[level, pl.ds(0, 7)])
        if level == TOP:
            break
        target = level + 1
        span, base, me = members(target)
        wide, deep = grid_of(span)
        values = full(level)
        for dx in ORDER[wide]:
            x = lax.rem(me // deep + dx, wide)
            group = pl.ds(x * deep, deep)
            total = dot(fold[target][level, group].reshape(deep * PAIR, WIDTH), values)
            total = total.reshape(deep, PAIR, PART)
            if target > 1:
                total = total + pre[target][group]
            part_out[target][group] = total.astype(BF16)
            for dy in ORDER[deep]:
                to = x * deep + lax.rem(lax.rem(me, deep) + dy, deep)
                if dx or dy:
                    send(
                        part_out[target].at[to],
                        part_in[target].at[me],
                        LEAF + target,
                        base + to,
                        row,
                    )
        part_in[target][me] = part_out[target][me]
        if level == 0:
            prepare_diag(2)
            prepare_fold(3)
            receive(RHS_X, rhs_in.at[0])
        elif level == 1:
            prepare_diag(4)
            prepare_fold_t(1)
        elif level == 2:
            prepare_diag(5)
            outputs(0)
            outputs(1)
        elif level == 3:
            outputs(2)
            prepare_fold_t(5)
        else:
            outputs(3)
            prepare_fold_t(2)
    solved = dot(twice[TOP], full(TOP))
    block = (solved * pair_mask(TOP)).astype(BF16).reshape(2, ROWS, PART)
    adj_out = fwd_out.at[pl.ds(LEVELS, LEVELS)]
    adj_out[0] = jnp.zeros((2, ROWS, PART), BF16)
    adj_out[TOP] = block
    send_gathered(TOP, block)
    for level in reversed(range(TOP)):
        upper = level + 1
        span, base, me = members(upper)
        if level == TOP - 1:
            outputs(TOP)
            for t in reversed(TARGETS):
                receive(FOLD_T + t, fold_t[t].at[:, 0])
        receive(B_LEAF + upper, gathered[upper].at[:, pl.ds(0, span - 1)])
        values = [gathered[upper][b].reshape(span * ROWS, PART) for b in range(2)]
        for dq in (2, 0):
            quarters = [lax.rem(quarter + dq + i, 4) for i in range(2)]
            total = None
            for b in range(2):
                side = jnp.concatenate([fold_t[upper][level, b, q] for q in quarters], axis=0)
                term = dot(side, values[b])
                total = term if total is None else total + term
            for i, q in enumerate(quarters):
                piece = total[i * 128 : (i + 1) * 128]
                if upper < TOP:
                    piece = piece + pulled_pre[level, q]
                pair_out[level, pl.ds(q * 2, 2)] = piece.astype(BF16).reshape(2, 2, ROWS, PART)
            for k in (4, 5, 6) if dq else (3, 2, 1, 7):
                to = lax.rem(z + k, CHIPS)
                if level > 0:
                    send(
                        pair_out.at[level, to],
                        pair_in.at[level, z],
                        B_Z + level,
                        leaf,
                        to * 2 + core,
                    )
                else:
                    for b in range(2):
                        send(
                            pair_out.at[0, to, b],
                            pair_in.at[0, z, core],
                            B_Z,
                            leaf,
                            to * 2 + b,
                        )
        if level > 0:
            pair_in[level, z] = pair_out[level, z]
        else:
            send(pair_out.at[0, z, other], pair_in.at[0, z, core], B_Z, leaf, sibling)
            pair_in[0, z, core] = pair_out[0, z, core]
        if level > 0:
            prepare_pulled(level - 1)
            receive(B_Z + level, pair_in.at[level, pl.ds(0, 7)])
            pulled = jnp.sum(pair_in[level].astype(F32), axis=0)
            mask = pair_mask(level).reshape(2, ROWS, 1)
            block = ((head[level] - pulled) * mask).astype(BF16)
            adj_out[level] = block
            send_gathered(level, block)
            if level == 1:
                send(fwd_out.at[:, other], fwd_in, FWD_X, leaf, sibling)
                receive(HEAD_X, head_in)
        else:
            receive(FWD_X, fwd_in)
            for out, part in ((fwd, 0), (adj, LEVELS)):
                for lv in range(LEVELS):
                    if part and not lv:
                        continue
                    for c in range(2):
                        block = jnp.where(core == c, fwd_out[part + lv, core], fwd_in[part + lv])
                        out[lv, 0, :, pl.ds(c * PART, PART)] = block
            receive(B_Z, pair_in.at[pl.ds(0, 5), pl.ds(0, 3), 0])
            pulled = jnp.sum(pair_in[0].astype(F32), axis=0)
            mask = row_mask(0, row * ROWS, ROWS)
            for c in range(2):
                ahead = jnp.where(core == c, head[0, core], head_in[...])
                adj[0, 0, :, pl.ds(c * PART, PART)] = ((ahead - pulled[c]) * mask).astype(BF16)
    for slot, ref in sends:
        wait(send_sem, slot, ref)


def scratch_shapes():
    vmem = pltpu.VMEM
    shapes = []
    shapes += [vmem((t, group_size(t), ROWS, WIDTH), BF16) for t in TARGETS]
    shapes += [vmem((t, group_size(t), 2, ROWS, WIDTH), BF16) for t in TARGETS]
    shapes += [vmem((t, 2, 4, 128, group_size(t) * ROWS), BF16) for t in TARGETS]
    shapes += [
        vmem((LEVELS, WIDTH, WIDTH), BF16),
        vmem((LEVELS, CHIPS, PAIR, WIDTH), BF16),
        vmem((LEVELS, PAIR, WIDTH), BF16),
    ]
    shapes += [vmem((group_size(t), PAIR, PART), F32) for t in TARGETS]
    shapes += [vmem((group_size(t), PAIR, PART), BF16) for t in TARGETS]
    shapes += [vmem((group_size(t), PAIR, PART), BF16) for t in TARGETS]
    shapes += [vmem((LEVELS, CHIPS, PAIR, PART), BF16)]
    shapes += [vmem((2, group_size(t), ROWS, PART), BF16) for t in TARGETS]
    shapes += [
        vmem((TOP, 4, 128, PART), F32),
        vmem((TOP, CHIPS, 2, ROWS, PART), BF16),
        vmem((TOP, CHIPS, 2, ROWS, PART), BF16),
        vmem((LEVELS, 2, ROWS, PART), F32),
        vmem((LEVELS, ROWS, COLUMNS), BF16),
        vmem((2, LEVELS, ROWS, PART), BF16),
        vmem((2, LEVELS, ROWS, PART), BF16),
        vmem((2 * LEVELS, 2, ROWS, PART), BF16),
        vmem((2 * LEVELS, ROWS, PART), BF16),
        vmem((ROWS, PART), F32),
        vmem((2, ROWS, PART), BF16),
        pltpu.SMEM((LEVELS,), jnp.int32),
        pltpu.SMEM((1, 178), jnp.int32),
        pltpu.SemaphoreType.DMA((SLOTS,)),
        pltpu.SemaphoreType.DMA((SLOTS,)),
        pltpu.SemaphoreType.DMA((24,)),
    ]
    return shapes


def shards(rhs, diag_inverse, factor, widths, structure):
    out = jax.ShapeDtypeStruct((LEVELS, 1, ROWS, COLUMNS), BF16)
    return pl.pallas_call(
        kernel,
        out_shape=(out, out),
        in_specs=[pl.BlockSpec(memory_space=pltpu.HBM)] * 5,
        out_specs=[pl.BlockSpec(memory_space=pltpu.VMEM)] * 2,
        scratch_shapes=scratch_shapes(),
        compiler_params=pltpu.CompilerParams(
            collective_id=0, has_side_effects=True, vmem_limit_bytes=56 * 2**20
        ),
    )(rhs, diag_inverse, factor, widths.reshape(LEVELS), structure)


def solution(mesh):
    placed = (
        P(None, "leaf", "row", None),
        P("leaf", None, None, None),
        P("leaf", None, "row", None),
        P(None, "leaf"),
        P("leaf", None),
    )
    return jax.shard_map(
        shards,
        mesh=mesh,
        in_specs=placed,
        out_specs=(P(None, "leaf", "row", None), P(None, "leaf", "row", None)),
        check_vma=False,
    )
```

time: 134 us -> 117 us (0.87)
  Pallas kernels: 130 us -> 113 us
    pallas_call x1, Pallas kernels: 130 us -> 113 us  [shards(): pl.pallas_call(kernel, out_shape=(out, out), in_specs=[pl.BlockSpec(memor...]
    unnamed x7 -> x2, local copies, waits for them, and re-layouts: 3.6 us -> 3.08 us
where the time goes in v2:
time: 117 us
  Pallas kernels  113 us (97%)
  local copies, waits for them, and re-layouts  3.08 us (3%)
    pallas_call x1, Pallas kernels, shards(): pl.pallas_call(kernel, out_shape=(out, out), in_specs=[pl.BlockSpec(memor...  113 us
    unnamed x2, local copies, waits for them, and re-layouts  3.08 us

profile of v2, /device:TPU:1, one launch (start us, length us, event | category | flops | bytes accessed | tf_op | source)
XLA Modules:
  0.0 116.8 jit_solution(9251830465011990094)
XLA Ops:
  0.6 113.0 %shard_map.68 = (bf16[6,1,32,256]{3,2,1,0:T(8,128)(2,1)}, bf16[6,1,32,256]{3,2,1,0:T(8,128)(2,1)}) custom-call(bf16[6,1,32,256]{3,2,1,0:T(8,128)(2,1)} %rhs_hbm.1, bf16[1,6,512,512]{3,2,1,0:T(8,128)(2,1)} %diag.1, bf16[1,178,32,512]{3,2,1,0:T(8,128)(2,1)} %factor.1, s32[6]{0:T(128)} %bitcast.1, s32[1,178]{1,0:T(1,128)} %structure_hbm.1), custom_call_target="tpu_custom_call" | custom-call | tf_op jit(solution)/shard_map/pallas_call | solution.py:465
  113.7 1.5 %copy.9 = bf16[6,1,32,256]{3,2,1,0:T(8,128)(2,1)} copy(bf16[6,1,32,256]{3,2,1,0:T(8,128)(2,1)} %get-tuple-element.4) | data formatting | bytes 196608
  115.2 1.5 %copy.10 = bf16[6,1,32,256]{3,2,1,0:T(8,128)(2,1)} copy(bf16[6,1,32,256]{3,2,1,0:T(8,128)(2,1)} %get-tuple-element.5) | data formatting | bytes 196608

commit v3 on v2

v3 whole, which is shorter than its diff:
```python
import jax
import jax.numpy as jnp
from jax import lax
from jax.experimental import pallas as pl
from jax.experimental.pallas import tpu as pltpu
from jax.sharding import PartitionSpec as P

MESH = pl.DeviceIdType.MESH
F32 = jnp.float32
BF16 = jnp.bfloat16
LEVELS = 6
LEAVES = 16
CHIPS = 8
ROWS = 32
PAIR = 2 * ROWS
WIDTH = 512
COLUMNS = 256
PART = COLUMNS // 2
TARGETS = tuple(range(1, LEVELS))
TOP = LEVELS - 1
Z_ORDER = (0, 1, 7, 2, 6, 3, 5, 4)
Z_SLOT = {d: i for i, d in enumerate(Z_ORDER)}
FAR_FIRST = Z_ORDER[:0:-1]


def group_size(level):
    return min(2**level, LEAVES)


def block_offsets():
    table, cursor = {}, 0
    for source in range(LEVELS):
        for target in range(source + 1, LEVELS):
            table[source, target] = cursor
            cursor += group_size(target)
    return table


OFFSETS = block_offsets()


def dot(a, b):
    return jnp.dot(a, b, preferred_element_type=F32)


def dot_nt(a, b):
    return lax.dot_general(a, b, (((1,), (1,)), ((), ())), preferred_element_type=F32)


ROW_Z, LEAF, B_LEAF, B_Z = (i * 2 * LEVELS for i in range(4))
FOLD, FOLD_T = 8 * LEVELS, 9 * LEVELS
RHS_X, FWD_X, HEAD_X = (10 * LEVELS + i for i in range(3))
SLOTS = 10 * LEVELS + 3


def ring(d, n):
    return min(d, n - d) if n > 2 else d


def extent(span):
    deep = min(span, 4)
    return span // deep, deep


def leaf_order(span):
    wide, deep = extent(span)
    steps = [(dx, dy) for dx in range(wide) for dy in range(deep)]
    return sorted(steps, key=lambda d: ring(d[0], wide) + ring(d[1], deep))


def leaf_back(span, step):
    wide, deep = extent(span)
    return leaf_order(span).index((-step[0] % wide, -step[1] % deep))


def kernel(rhs_hbm, diag, factor, widths_hbm, structure_hbm, fwd, adj, *scratch):
    scratch = list(scratch)

    def take(n):
        out = scratch[:n]
        del scratch[:n]
        return out

    per_target = lambda: dict(zip(TARGETS, take(len(TARGETS))))
    blocks, sorted_blocks, fold, fold_t = per_target(), per_target(), per_target(), per_target()
    dm, dm_t, own_rows, twice, turned = take(5)
    pre, part_out, part_in = per_target(), per_target(), per_target()
    (resid,) = take(1)
    gathered = per_target()
    pulled_pre, pair_out, pair_in, head = take(4)
    rhs, rhs_out, rhs_in, fwd_out, fwd_in, head_in, first_out, whole = take(8)
    widths, structure = take(2)
    send_sem, recv_sem, load_sem, out_sem = take(4)

    leaf = lax.axis_index("leaf")
    row = lax.axis_index("row")
    z, core = row // 2, lax.rem(row, 2)
    other = 1 - core
    sibling = z * 2 + other

    barrier = pltpu.get_barrier_semaphore()

    def greet(leaf_to, row_to):
        pl.semaphore_signal(barrier, inc=1, device_id=(leaf_to, row_to), device_id_type=MESH)

    for k in FAR_FIRST:
        for c in range(2):
            greet(leaf, lax.rem(z + k, CHIPS) * 2 + c)
    for k in range(1, LEAVES):
        greet(lax.rem(leaf + k, LEAVES), row)
    greet(leaf, sibling)

    loads = {}

    def load(name, src, dst):
        loads[name] = pltpu.make_async_copy(src, dst, load_sem.at[len(loads)])
        loads[name].start()

    load("widths", widths_hbm, widths)
    load("rhs", rhs_hbm.at[:, 0], rhs)
    load("structure", structure_hbm, structure)
    load("diag", diag.at[0], dm)
    for t in TARGETS:
        for s in range(t):
            load((s, t), factor.at[0, pl.ds(OFFSETS[s, t], group_size(t))], blocks[t].at[s])

    sends = []

    def send(src, dst, slot, leaf_to, row_to):
        pltpu.make_async_remote_copy(
            src_ref=src,
            dst_ref=dst,
            send_sem=send_sem.at[slot],
            recv_sem=recv_sem.at[slot],
            device_id=(leaf_to, row_to),
            device_id_type=MESH,
        ).start()

    def wait(sem, slot, ref):
        pltpu.make_async_copy(ref, ref, sem.at[slot]).wait()

    def receive(slot, ref):
        wait(recv_sem, slot, ref)
        sends.append((slot, ref))

    def member(span, step):
        wide, deep = extent(span)
        me = lax.rem(leaf, span)
        x = lax.rem(me // deep + step[0], wide)
        return x * deep + lax.rem(lax.rem(me, deep) + step[1], deep)

    def leaf_of(span, step):
        return leaf // span * span + member(span, step)

    def row_mask(level, first, count):
        rows = first + lax.broadcasted_iota(jnp.int32, (count, 1), 0)
        return (rows < widths[level]).astype(F32)

    def pair_mask(level):
        return row_mask(level, z * PAIR, PAIR)

    def prepare_diag(s):
        masked = (dm[s].astype(F32) * row_mask(s, 0, WIDTH)).astype(BF16)
        turned[...] = masked.T.reshape(CHIPS, PAIR, WIDTH)
        for i, d in enumerate(Z_ORDER):
            dm_t[s, i] = turned[lax.rem(z + d, CHIPS)]
        everything = dm_t[s].reshape(WIDTH, WIDTH)
        twice[s] = dot_nt(dm_t[s, 0], everything).astype(BF16)
        wanted = z * PAIR + lax.broadcasted_iota(jnp.int32, (PAIR, WIDTH), 0)
        at = lax.broadcasted_iota(jnp.int32, (PAIR, WIDTH), 1)
        chosen = (at == wanted).astype(F32).astype(BF16)
        own_rows[s] = dot_nt(chosen, everything).astype(BF16)

    def sort_blocks(t):
        for s in range(t):
            loads[s, t].wait()
        span = group_size(t)

        def scale(s, carry):
            first = OFFSETS[0, t]
            for later in range(1, t):
                first = jnp.where(s == later, OFFSETS[later, t], first)
            for i, step in enumerate(leaf_order(span)):
                p = member(span, step)
                w = structure[0, first + p].astype(F32)
                sorted_blocks[t][s, i] = (blocks[t][s, p].astype(F32) * w).astype(BF16)
            return carry

        lax.fori_loop(0, t, scale, 0)

    def prepare_fold(t):
        sort_blocks(t)
        span = group_size(t)

        def step(s, carry):
            flat = sorted_blocks[t][s].reshape(span * ROWS, WIDTH)
            for k in range(2):
                part = dot_nt(flat, dm_t[s, pl.ds(k * 4, 4)].reshape(256, WIDTH)).astype(BF16)
                fold[t][s, :, core, :, k * 256 : (k + 1) * 256] = part.reshape(span, ROWS, 256)
            return carry

        lax.fori_loop(0, t, step, 0)
        mine = fold[t].at[:, :, core]
        send(mine, mine, FOLD + t, leaf, sibling)

    def prepare_fold_t(t):
        height = group_size(t) * ROWS

        def step(s, carry):
            flat = sorted_blocks[t][s].reshape(height, WIDTH)
            for m in range(2):
                part = dot_nt(dm_t[s, pl.ds(m * 4, 4)].reshape(256, WIDTH), flat)
                fold_t[t][s, core, m] = part.astype(BF16)
            return carry

        lax.fori_loop(0, t, step, 0)
        mine = fold_t[t].at[:, core]
        send(mine, mine, FOLD_T + t, leaf, sibling)

    def prepare_third():
        prepare_diag(2)
        prepare_fold(3)

    def full(level):
        return resid[level].reshape(WIDTH, PART)

    def prepare_pre(t):
        receive(FOLD + t, fold[t].at[:, :, 0])
        height = group_size(t) * PAIR
        total = None
        for s in range(t - 1):
            term = dot(fold[t][s].reshape(height, WIDTH), full(s))
            total = term if total is None else total + term
        if total is not None:
            pre[t][...] = total

    def outputs(level):
        fwd_out[level] = dot(own_rows[level], full(level)).astype(BF16).reshape(2, ROWS, PART)
        head[level] = dot(twice[level], full(level)).reshape(2, ROWS, PART)

    def prepare_pulled(s):
        for m in range(2):
            total = None
            for t in range(s + 2, LEVELS):
                for b in range(2):
                    values = gathered[t][b].reshape(group_size(t) * ROWS, PART)
                    term = dot(fold_t[t][s, b, m], values)
                    total = term if total is None else total + term
            pulled_pre[s, m] = total

    def send_gathered(level, block):
        span = group_size(level)
        gathered[level][:, 0] = block
        for step in reversed(leaf_order(span)[1:]):
            there = leaf_back(span, step)
            send(
                gathered[level].at[:, 0],
                gathered[level].at[:, there],
                B_LEAF + 2 * level + (2 * there >= span),
                leaf_of(span, step),
                row,
            )

    loads["widths"].wait()
    loads["rhs"].wait()
    first = (rhs[0].astype(F32) * row_mask(0, row * ROWS, ROWS)).astype(BF16)
    for c in range(2):
        first_out[c] = first[:, c * PART : (c + 1) * PART]
        rhs_out[c] = rhs[:, :, c * PART : (c + 1) * PART]
    mine = pl.ds(pl.multiple_of(core * ROWS, ROWS), ROWS)
    resid[0, 0, mine] = first_out[core]
    pl.semaphore_wait(barrier, LEAVES + 14)
    for d in FAR_FIRST:
        there = resid.at[0, Z_SLOT[-d % CHIPS], mine]
        for c in range(2):
            to = lax.rem(z + d, CHIPS) * 2 + c
            send(first_out.at[c], there, ROW_Z + (Z_SLOT[-d % CHIPS] > 3), leaf, to)
    send(first_out.at[other], resid.at[0, 0, mine], ROW_Z, leaf, sibling)
    send(rhs_out.at[other], rhs_in.at[core], RHS_X, leaf, sibling)
    rhs_in[core] = rhs_out[core]

    for level in range(LEVELS):
        if level > 0:
            span = group_size(level)
            near = span // 2
            value = rhs_in[:, level].reshape(PAIR, PART).astype(F32)
            if near > 1:
                receive(LEAF + 2 * level, part_in[level].at[pl.ds(0, near - 1)])
            value = value - jnp.sum(part_in[level][:near].astype(F32), axis=0)
            receive(LEAF + 2 * level + 1, part_in[level].at[pl.ds(0, near)])
            value = value - jnp.sum(part_in[level][near:].astype(F32), axis=0)
            resid[level, 0] = (value * pair_mask(level)).astype(BF16)
            for d in FAR_FIRST:
                there = Z_SLOT[-d % CHIPS]
                send(
                    resid.at[level, 0],
                    resid.at[level, there],
                    ROW_Z + 2 * level + (there > 3),
                    leaf,
                    lax.rem(z + d, CHIPS) * 2 + core,
                )
        if level == 0:
            loads["diag"].wait()
            loads["structure"].wait()
            prepare_diag(0)
            prepare_fold(1)
            prepare_diag(1)
            prepare_fold(2)
        elif level == 1:
            prepare_diag(3)
            prepare_fold(4)
        elif level == 2:
            prepare_fold(5)
        elif level == 3:
            prepare_fold_t(4)
        elif level == 4:
            prepare_fold_t(3)
        else:
            outputs(4)
            send(head.at[0, other], head_in, HEAD_X, leaf, sibling)
        target = level + 1
        if level < TOP:
            prepare_pre(target)
            span = group_size(target)
            near = span // 2
            height = near * PAIR
        for k in range(2):
            if level > 0:
                receive(ROW_Z + 2 * level + k, resid.at[level, pl.ds(0, 3 + k)])
            elif k:
                receive(ROW_Z + 1, resid.at[pl.ds(0, 4), pl.ds(0, 2), pl.ds(0, ROWS)])
            else:
                receive(ROW_Z, resid.at[0, pl.ds(0, 7), pl.ds(0, ROWS)])
            if level == TOP:
                continue
            if level == 0 and k:
                pl.when(core == 1)(prepare_third)
            values = resid[level, k * 4 : k * 4 + 4].reshape(256, PART)
            for m in (1, 0):
                rows = slice(m * height, (m + 1) * height)
                half = fold[target][level, m * near : (m + 1) * near]
                half = half.reshape(height, WIDTH)[:, k * 256 : (k + 1) * 256]
                total = dot(half, values)
                if target > 1 or k:
                    total = total + pre[target][rows]
                if k == 0:
                    pre[target][rows] = total
                    continue
                total = total.astype(BF16).reshape(near, PAIR, PART)
                part_out[target][m * near : (m + 1) * near] = total
                for i in reversed(range(max(m * near, 1), (m + 1) * near)):
                    step = leaf_order(span)[i]
                    there = leaf_back(span, step)
                    send(
                        part_out[target].at[i],
                        part_in[target].at[there],
                        LEAF + 2 * target + (there >= near),
                        leaf_of(span, step),
                        row,
                    )
                if m == 0:
                    part_in[target][0] = part_out[target][0]
        if level == 0:
            pl.when(core == 0)(prepare_third)
            receive(RHS_X, rhs_in.at[0])
        elif level == 1:
            prepare_diag(4)
            prepare_fold_t(1)
        elif level == 2:
            prepare_diag(5)
            outputs(0)
            outputs(1)
        elif level == 3:
            outputs(2)
            prepare_fold_t(5)
        elif level == 4:
            outputs(3)
            prepare_fold_t(2)
    solved = dot(twice[TOP], full(TOP))
    block = (solved * pair_mask(TOP)).astype(BF16).reshape(2, ROWS, PART)
    adj_out = fwd_out.at[pl.ds(LEVELS, LEVELS)]
    adj_out[0] = jnp.zeros((2, ROWS, PART), BF16)
    adj_out[TOP] = block
    send_gathered(TOP, block)
    for level in reversed(range(TOP)):
        upper = level + 1
        span = group_size(upper)
        near = span // 2
        if level == TOP - 1:
            outputs(TOP)
            for t in reversed(TARGETS):
                receive(FOLD_T + t, fold_t[t].at[:, 0])
        begun = upper < TOP
        for k in range(2):
            if k:
                receive(B_LEAF + 2 * upper + 1, gathered[upper].at[:, pl.ds(0, near)])
            elif near > 1:
                receive(B_LEAF + 2 * upper, gathered[upper].at[:, pl.ds(0, near - 1)])
            if span >= 8:
                first, count = k * near, near
            elif k:
                first, count = 0, span
            else:
                continue
            for m in (1, 0):
                total = None
                for b in range(2):
                    values = gathered[upper][b, first : first + count]
                    half = fold_t[upper][
                        level, b, m, :, first * ROWS : (first + count) * ROWS
                    ]
                    term = dot(half, values.reshape(count * ROWS, PART))
                    total = term if total is None else total + term
                if begun:
                    total = total + pulled_pre[level, m]
                if k == 0:
                    pulled_pre[level, m] = total
                    continue
                pair_out[level, m * 4 : m * 4 + 4] = total.astype(BF16).reshape(4, 2, ROWS, PART)
                for d in reversed(Z_ORDER[max(m * 4, 1) : m * 4 + 4]):
                    i, there = Z_SLOT[d], Z_SLOT[-d % CHIPS]
                    to = lax.rem(z + d, CHIPS)
                    slot = B_Z + 2 * level + (there > 3)
                    if level > 0:
                        send(
                            pair_out.at[level, i],
                            pair_in.at[level, there],
                            slot,
                            leaf,
                            to * 2 + core,
                        )
                        continue
                    for b in range(2):
                        landing = pair_in.at[0, there, core]
                        send(pair_out.at[0, i, b], landing, slot, leaf, to * 2 + b)
            begun = True
        if level > 0:
            pair_in[level, 0] = pair_out[level, 0]
            prepare_pulled(level - 1)
            value = head[level]
            receive(B_Z + 2 * level, pair_in.at[level, pl.ds(0, 3)])
            value = value - jnp.sum(pair_in[level, :4].astype(F32), axis=0)
            receive(B_Z + 2 * level + 1, pair_in.at[level, pl.ds(0, 4)])
            value = value - jnp.sum(pair_in[level, 4:].astype(F32), axis=0)
            block = (value * pair_mask(level).reshape(2, ROWS, 1)).astype(BF16)
            adj_out[level] = block
            send_gathered(level, block)
            if level == 1:
                send(fwd_out.at[:, other], fwd_in, FWD_X, leaf, sibling)
                receive(HEAD_X, head_in)
            continue
        send(pair_out.at[0, 0, other], pair_in.at[0, 0, core], B_Z, leaf, sibling)
        pair_in[0, 0, core] = pair_out[0, 0, core]
        receive(FWD_X, fwd_in)
        for i in range(2 * LEVELS):
            if i == LEVELS:
                continue
            for c in range(2):
                block = jnp.where(core == c, fwd_out[i, core], fwd_in[i])
                whole[i, :, c * PART : (c + 1) * PART] = block
        stores = [
            (whole.at[pl.ds(0, LEVELS)], fwd.at[:, 0]),
            (whole.at[pl.ds(LEVELS + 1, TOP)], adj.at[pl.ds(1, TOP), 0]),
            (whole.at[LEVELS], adj.at[0, 0]),
        ]
        stores = [pltpu.make_async_copy(*pair, out_sem.at[i]) for i, pair in enumerate(stores)]
        stores[0].start()
        stores[1].start()
        receive(B_Z, pair_in.at[0, pl.ds(0, 7), 0])
        near_sum = jnp.sum(pair_in[0, :4].astype(F32), axis=0)
        receive(B_Z + 1, pair_in.at[0, pl.ds(0, 4)])
        pulled = near_sum + jnp.sum(pair_in[0, 4:].astype(F32), axis=0)
        mask = row_mask(0, row * ROWS, ROWS)
        for c in range(2):
            ahead = jnp.where(core == c, head[0, core], head_in[...])
            block = ((ahead - pulled[c]) * mask).astype(BF16)
            whole[LEVELS, :, c * PART : (c + 1) * PART] = block
        stores[2].start()
        for slot, ref in sends:
            wait(send_sem, slot, ref)
        for store in stores:
            store.wait()


def scratch_shapes():
    vmem = pltpu.VMEM
    shapes = []
    for _ in range(2):
        shapes += [vmem((t, group_size(t), ROWS, WIDTH), BF16) for t in TARGETS]
    shapes += [vmem((t, group_size(t), 2, ROWS, WIDTH), BF16) for t in TARGETS]
    shapes += [vmem((t, 2, 2, 256, group_size(t) * ROWS), BF16) for t in TARGETS]
    shapes += [
        vmem((LEVELS, WIDTH, WIDTH), BF16),
        vmem((LEVELS, CHIPS, PAIR, WIDTH), BF16),
        vmem((LEVELS, PAIR, WIDTH), BF16),
        vmem((LEVELS, PAIR, WIDTH), BF16),
        vmem((CHIPS, PAIR, WIDTH), BF16),
    ]
    shapes += [vmem((group_size(t) * PAIR, PART), F32) for t in TARGETS]
    shapes += [vmem((group_size(t), PAIR, PART), BF16) for t in TARGETS]
    shapes += [vmem((group_size(t), PAIR, PART), BF16) for t in TARGETS]
    shapes += [vmem((LEVELS, CHIPS, PAIR, PART), BF16)]
    shapes += [vmem((2, group_size(t), ROWS, PART), BF16) for t in TARGETS]
    shapes += [
        vmem((TOP, 2, 256, PART), F32),
        vmem((TOP, CHIPS, 2, ROWS, PART), BF16),
        vmem((TOP, CHIPS, 2, ROWS, PART), BF16),
        vmem((LEVELS, 2, ROWS, PART), F32),
        vmem((LEVELS, ROWS, COLUMNS), BF16),
        vmem((2, LEVELS, ROWS, PART), BF16),
        vmem((2, LEVELS, ROWS, PART), BF16),
        vmem((2 * LEVELS, 2, ROWS, PART), BF16),
        vmem((2 * LEVELS, ROWS, PART), BF16),
        vmem((ROWS, PART), F32),
        vmem((2, ROWS, PART), BF16),
        vmem((2 * LEVELS, ROWS, COLUMNS), BF16),
        pltpu.SMEM((LEVELS,), jnp.int32),
        pltpu.SMEM((1, 178), jnp.int32),
        pltpu.SemaphoreType.DMA((SLOTS,)),
        pltpu.SemaphoreType.DMA((SLOTS,)),
        pltpu.SemaphoreType.DMA((24,)),
        pltpu.SemaphoreType.DMA((3,)),
    ]
    return shapes


def deliver(a, b, a_out, b_out):
    a_out[...] = a[...]
    b_out[...] = b[...]


def shards(rhs, diag_inverse, factor, widths, structure):
    out = jax.ShapeDtypeStruct((LEVELS, 1, ROWS, COLUMNS), BF16)
    hbm = pl.BlockSpec(memory_space=pltpu.HBM)
    solved = pl.pallas_call(
        kernel,
        out_shape=(out, out),
        in_specs=[hbm] * 5,
        out_specs=[hbm] * 2,
        scratch_shapes=scratch_shapes(),
        compiler_params=pltpu.CompilerParams(
            collective_id=0, has_side_effects=True, vmem_limit_bytes=58 * 2**20
        ),
    )(rhs, diag_inverse, factor, widths.reshape(LEVELS), structure)
    vmem = pl.BlockSpec(memory_space=pltpu.VMEM)
    return pl.pallas_call(
        deliver,
        out_shape=(out, out),
        in_specs=[vmem] * 2,
        out_specs=[vmem] * 2,
    )(*solved)


def solution(mesh):
    placed = (
        P(None, "leaf", "row", None),
        P("leaf", None, None, None),
        P("leaf", None, "row", None),
        P(None, "leaf"),
        P("leaf", None),
    )
    return jax.shard_map(
        shards,
        mesh=mesh,
        in_specs=placed,
        out_specs=(P(None, "leaf", "row", None), P(None, "leaf", "row", None)),
        check_vma=False,
    )
```

time: 117 us -> 115 us (0.983)
  local copies, waits for them, and re-layouts: 3.08 us -> 0 us
    unnamed x2 -> x0, local copies, waits for them, and re-layouts: 3.08 us -> none
    pallas_call x1 -> x2, Pallas kernels: 113 us -> 114 us  [the longest x1 113 us: shards(): pl.pallas_call(kernel, out_shape=(out, out), in_specs=[hbm] * 5, out_spec...]
where the time goes in v3:
time: 115 us
  Pallas kernels  114 us (99%)
    pallas_call x1, Pallas kernels, shards(): pl.pallas_call(kernel, out_shape=(out, out), in_specs=[hbm] * 5, out_spec...  113 us

profile of v3, /device:TPU:1, one launch (start us, length us, event | category | flops | bytes accessed | tf_op | source)
XLA Modules:
  0.0 115.0 jit_solution(385005384007282493)
XLA Ops:
  0.6 112.8 %shard_map.68 = (bf16[6,1,32,256]{3,2,1,0:T(8,128)(2,1)}, bf16[6,1,32,256]{3,2,1,0:T(8,128)(2,1)}) custom-call(bf16[6,1,32,256]{3,2,1,0:T(8,128)(2,1)} %rhs_hbm.1, bf16[1,6,512,512]{3,2,1,0:T(8,128)(2,1)} %diag.1, bf16[1,178,32,512]{3,2,1,0:T(8,128)(2,1)} %factor.1, s32[6]{0:T(128)} %bitcast.1, s32[1,178]{1,0:T(1,128)} %structure_hbm.1), custom_call_target="tpu_custom_call" | custom-call | tf_op jit(solution)/shard_map/pallas_call | solution.py:535
  113.4 1.6 %shard_map.69 = (bf16[6,1,32,256]{3,2,1,0:T(8,128)(2,1)}, bf16[6,1,32,256]{3,2,1,0:T(8,128)(2,1)}) custom-call(bf16[6,1,32,256]{3,2,1,0:T(8,128)(2,1)} %get-tuple-element.4.a, bf16[6,1,32,256]{3,2,1,0:T(8,128)(2,1)} %get-tuple-element.5.b), custom_call_target="tpu_custom_call" | custom-call | tf_op jit(solution)/shard_map/pallas_call | solution.py:546

commit v4 on v3

--- a/solution.py
+++ b/solution.py
@@ -98,6 +98,15 @@
     other = 1 - core
     sibling = z * 2 + other
 
+    loads = {}
+
+    def load(name, src, dst):
+        loads[name] = pltpu.make_async_copy(src, dst, load_sem.at[len(loads)])
+        loads[name].start()
+
+    load("widths", widths_hbm, widths)
+    load("rhs", rhs_hbm.at[:, 0], rhs)
+
     barrier = pltpu.get_barrier_semaphore()
 
     def greet(leaf_to, row_to):
@@ -110,14 +119,6 @@
         greet(lax.rem(leaf + k, LEAVES), row)
     greet(leaf, sibling)
 
-    loads = {}
-
-    def load(name, src, dst):
-        loads[name] = pltpu.make_async_copy(src, dst, load_sem.at[len(loads)])
-        loads[name].start()
-
-    load("widths", widths_hbm, widths)
-    load("rhs", rhs_hbm.at[:, 0], rhs)
     load("structure", structure_hbm, structure)
     load("diag", diag.at[0], dm)
     for t in TARGETS:
@@ -138,6 +139,11 @@
 
     def wait(sem, slot, ref):
         pltpu.make_async_copy(ref, ref, sem.at[slot]).wait()
+
+    def drain():
+        for slot, ref in sends:
+            wait(send_sem, slot, ref)
+        sends.clear()
 
     def receive(slot, ref):
         wait(recv_sem, slot, ref)
@@ -466,6 +472,7 @@
         stores = [pltpu.make_async_copy(*pair, out_sem.at[i]) for i, pair in enumerate(stores)]
         stores[0].start()
         stores[1].start()
+        drain()
         receive(B_Z, pair_in.at[0, pl.ds(0, 7), 0])
         near_sum = jnp.sum(pair_in[0, :4].astype(F32), axis=0)
         receive(B_Z + 1, pair_in.at[0, pl.ds(0, 4)])
@@ -476,8 +483,7 @@
             block = ((ahead - pulled[c]) * mask).astype(BF16)
             whole[LEVELS, :, c * PART : (c + 1) * PART] = block
         stores[2].start()
-        for slot, ref in sends:
-            wait(send_sem, slot, ref)
+        drain()
         for store in stores:
             store.wait()
 

time: 115 us -> 115 us (level)
  no operation moved by 1% of the time
where the time goes in v4:
time: 115 us
  Pallas kernels  114 us (99%)
    pallas_call x1, Pallas kernels, shards(): pl.pallas_call(kernel, out_shape=(out, out), in_specs=[hbm] * 5, out_spec...  113 us

profile of v4, /device:TPU:1, one launch (start us, length us, event | category | flops | bytes accessed | tf_op | source)
XLA Modules:
  0.0 115.0 jit_solution(5385956030196788633)
XLA Ops:
  0.6 112.8 %shard_map.68 = (bf16[6,1,32,256]{3,2,1,0:T(8,128)(2,1)}, bf16[6,1,32,256]{3,2,1,0:T(8,128)(2,1)}) custom-call(bf16[6,1,32,256]{3,2,1,0:T(8,128)(2,1)} %rhs_hbm.1, bf16[1,6,512,512]{3,2,1,0:T(8,128)(2,1)} %diag.1, bf16[1,178,32,512]{3,2,1,0:T(8,128)(2,1)} %factor.1, s32[6]{0:T(128)} %bitcast.1, s32[1,178]{1,0:T(1,128)} %structure_hbm.1), custom_call_target="tpu_custom_call" | custom-call | tf_op jit(solution)/shard_map/pallas_call | solution.py:541
  113.4 1.6 %shard_map.69 = (bf16[6,1,32,256]{3,2,1,0:T(8,128)(2,1)}, bf16[6,1,32,256]{3,2,1,0:T(8,128)(2,1)}) custom-call(bf16[6,1,32,256]{3,2,1,0:T(8,128)(2,1)} %get-tuple-element.4.a, bf16[6,1,32,256]{3,2,1,0:T(8,128)(2,1)} %get-tuple-element.5.b), custom_call_target="tpu_custom_call" | custom-call | tf_op jit(solution)/shard_map/pallas_call | solution.py:552
